TPU v7x, 32 devices: a whole 2x2x4 slice. The times are simulated.
32 devices in a mesh: img: 8 (over y, x, core), ch: 4 (over z).
Axes of the slice: x: 2, y: 2, z: 4, core: 2. Of those that a mesh axis runs over, the one named last changes fastest.
Arguments:
- features: bfloat16 [64, 256, 256], P('img', 'ch'), may hold values from -8 to 8
- labels: int32 [64], P('img'), may hold values from 0 to 9
- groups: int32 [64], P('img'), may hold values from 0 to 3, as said below
- widths: int32 [4], replicated, may hold values from 1 to 4, as said below
- entry_conv: float32 [2304, 256], P('img', 'ch'), may hold values from -0.2625 to 0.2625
- entry_moment: float32 [2304, 256], P('img', 'ch'), may hold values from -48 to 48
- entry_square: float32 [2304, 256], P('img', 'ch'), may hold values from 5.89824 to 23.59296
- exit_conv: float32 [2304, 256], P('img', 'ch'), may hold values from -0.2625 to 0.2625
- exit_moment: float32 [2304, 256], P('img', 'ch'), may hold values from -64 to 64
- exit_square: float32 [2304, 256], P('img', 'ch'), may hold values from 10.48576 to 41.94304
- bypass_conv: float32 [256, 256], P('img', 'ch'), may hold values from -0.78125 to 0.78125
- bypass_moment: float32 [256, 256], P('img', 'ch'), may hold values from -192 to 192
- bypass_square: float32 [256, 256], P('img', 'ch'), may hold values from 95.0272 to 376.832
- norm_affine: float32 [23, 256], P(None, 'ch'), may hold values from -1.25 to 1.75
- norm_moment: float32 [23, 256], P(None, 'ch'), may hold values from -128 to 128
- norm_square: float32 [23, 256], P(None, 'ch'), may hold values from 0.32768 to 262.144
- cotangent: bfloat16 [64, 256, 1024], P('img', 'ch'), may hold values from -6 to 6
Outputs:
- block_output: bfloat16 [64, 256, 1024], P('img', 'ch')
- input_gradient: float32 [64, 256, 256], P('img', 'ch')
- entry_first: float32 [2304, 256], P('img', 'ch')
- entry_second: float32 [2304, 256], P('img', 'ch')
- entry_weight: float32 [2304, 256], P('img', 'ch')
- exit_first: float32 [2304, 256], P('img', 'ch')
- exit_second: float32 [2304, 256], P('img', 'ch')
- exit_weight: float32 [2304, 256], P('img', 'ch')
- bypass_first: float32 [256, 256], P('img', 'ch')
- bypass_second: float32 [256, 256], P('img', 'ch')
- bypass_weight: float32 [256, 256], P('img', 'ch')
- affine_first: float32 [23, 256], P(None, 'ch')
- affine_second: float32 [23, 256], P(None, 'ch')
- affine_values: float32 [23, 256], P(None, 'ch')
- trust_norms: float32 [3, 3], replicated
Inputs may be any that keep to these rules, and one draw needn't show every extreme that they name: `groups`: each of the 4 micro-batches holds exactly 16 images. `widths`: every value from 1 to 4 occurs.
All inputs are finite; a program needn't handle non-finite values.
Results may differ from a plain program's by a relative error of at most 0.0075.
Values may be sent and summed in bfloat16 or wider, within the bound.
A program may use at most 128 MiB of HBM per device.

v0:
```python
import functools
import math
from types import SimpleNamespace

import jax
import jax.numpy as jnp
from jax import lax
from jax.experimental import pallas as pl
from jax.experimental.pallas import tpu as pltpu
from jax.sharding import PartitionSpec as P

LEVELS = 4
STEP = 5
NORM_EPSILON = 1e-05
ADAM_EPSILON = 1e-06
MOMENT_DECAY = 0.9
SQUARE_DECAY = 0.999
WEIGHT_DECAY = 0.01
MATRIX_RATE = 0.3
AFFINE_RATE = 0.2

OUTER = 8
VMEM_LIMIT = 56 * 1024 * 1024
BF16 = jnp.bfloat16
F32 = jnp.float32
MESH = pl.DeviceIdType.MESH
PARTS = ("s1", "r1", "s2", "r2", "s3", "r3")


def nn(left, right):
    return lax.dot_general(left, right, (((1,), (0,)), ((), ())), preferred_element_type=F32)


def nt(left, right):
    return lax.dot_general(left, right, (((1,), (1,)), ((), ())), preferred_element_type=F32)


def tn(left, right):
    return lax.dot_general(left, right, (((0,), (0,)), ((), ())), preferred_element_type=F32)


def flip(index, mask):
    result = index
    for bit in range(3):
        if (mask >> bit) & 1:
            digit = lax.rem(lax.div(index, 1 << bit), 2)
            result = result + (1 - 2 * digit) * (1 << bit)
    return result


def sigmoid(value):
    return 0.5 * jnp.tanh(0.5 * value) + 0.5


def iota(shape, axis):
    return lax.broadcasted_iota(jnp.int32, shape, axis)


def to_bf16(condition):
    return jnp.where(condition, 1.0, 0.0).astype(BF16)


def pick_row(table, index):
    hit = iota(table.shape, 0) == index
    return jnp.sum(jnp.where(hit, table, 0.0), axis=0, keepdims=True)


def place_row(row, index, rows):
    hit = iota((rows, row.shape[1]), 0) == index
    return jnp.where(hit, row, 0.0)


def colsum(value):
    return jnp.sum(value, axis=0, keepdims=True)


def adam_update(grad, moment, square):
    moment_new = MOMENT_DECAY * moment + (1.0 - MOMENT_DECAY) * grad
    square_new = SQUARE_DECAY * square + (1.0 - SQUARE_DECAY) * grad * grad
    direction = (
        moment_new
        / (1.0 - MOMENT_DECAY**STEP)
        / (jnp.sqrt(square_new / (1.0 - SQUARE_DECAY**STEP)) + ADAM_EPSILON)
    )
    return (moment_new, square_new, direction)


def total(value):
    return jnp.sum(jnp.sum(value, axis=1, keepdims=True), axis=0, keepdims=True)


def main_kernel(cfg, *refs):
    r = SimpleNamespace(**dict(zip(cfg.names, refs)))
    inner, n_ch, batch, local = cfg.inner, cfg.n_ch, cfg.batch, cfg.local
    classes, count = cfg.classes, cfg.count
    per = batch // n_ch
    chans = local * n_ch
    rows, small = cfg.rows, cfg.small
    tail = (rows - 256) // 2
    hw, hs = rows // 2, small // 2
    slots = SimpleNamespace(remote=0, local=0)

    img = lax.axis_index("img")
    me = lax.axis_index("ch")
    block = lax.div(img, inner)
    within = lax.rem(img, inner)
    core = lax.rem(block, 2)
    plane = lax.div(block, 2)
    partner = flip(block, 1)

    def dev(block_id, within_id, ch_id):
        return (block_id * inner + within_id, ch_id)

    pending = []

    def post(src, dst, landed, peer):
        slot = slots.remote
        slots.remote = slot + 1
        copy = pltpu.make_async_remote_copy(
            src_ref=src,
            dst_ref=dst,
            send_sem=r.send.at[slot],
            recv_sem=r.recv.at[slot],
            device_id=peer,
            device_id_type=MESH,
        )
        copy.start()
        pending.append(copy.wait_send)
        arrival = pltpu.make_async_remote_copy(
            src_ref=landed,
            dst_ref=landed,
            send_sem=r.send.at[slot],
            recv_sem=r.recv.at[slot],
            device_id=peer,
            device_id_type=MESH,
        )
        return arrival.wait_recv

    def here(src, dst):
        slot = slots.local
        slots.local = slot + 1
        copy = pltpu.make_async_copy(src, dst, r.lsem.at[slot])
        copy.start()
        return copy.wait

    outer_peers = [flip(block, mask) for mask in range(1, OUTER)]
    ch_peers = [flip(me, mask) for mask in range(1, n_ch)]
    inner_pairs = [
        (lax.rem(within + step, inner), lax.rem(within + inner - step, inner))
        for step in range(1, inner)
    ]
    up, down, far = (lax.rem(me + step, n_ch) for step in (1, 3, 2))
    up_peer, down_peer = dev(block, within, up), dev(block, within, down)

    class Ring:
        def __init__(self, source, target, passing):
            self.target, self.passing = target, passing
            self.waits = []
            self.early = [
                post(source(far, 0), passing.at[0], passing.at[0], up_peer),
                post(source(far, 1), passing.at[1], passing.at[1], down_peer),
            ]
            for im in range(per):
                self.waits += [
                    post(source(up, im), target(me, im), target(down, im), up_peer),
                    post(source(down, im), target(me, im), target(up, im), down_peer),
                ]

        def forward(self):
            self.early[0]()
            self.waits.append(
                post(self.passing.at[0], self.target(down, 0), self.target(far, 0), up_peer)
            )
            self.early[1]()
            self.waits.append(
                post(self.passing.at[1], self.target(up, 1), self.target(far, 1), down_peer)
            )

        def settle(self):
            for wait in self.waits:
                wait()

    barrier = pltpu.get_barrier_semaphore()
    everyone = [dev(peer, within, me) for peer in outer_peers]
    everyone += [dev(block, within, peer) for peer in ch_peers]
    everyone += [dev(block, peer, me) for peer, _ in inner_pairs]
    for peer in everyone:
        pl.semaphore_signal(barrier, inc=1, device_id=peer, device_id_type=MESH)

    got_entry = here(r.entry, r.entry_v)
    got_features = here(r.features, r.fown)
    got_exit = here(r.exit, r.exit_v)
    got_bypass = here(r.bypass, r.bypass_v)
    got_affine = here(r.affine, r.affine_v)
    got_cot = here(r.cotangent, r.cown)
    states = ((r.entry_m, r.entry_q), (r.exit_m, r.exit_q), (r.bypass_m, r.bypass_q)) if inner == 1 else ()
    held = [
        (here(m, getattr(r, v + "m")), here(q, getattr(r, v + "q")))
        for (m, q), v in zip(states, ("v1", "v2", "vs"))
    ]

    s_row, s_col = iota((hw, 384), 0), iota((hw, 384), 1)
    pick_first = to_bf16(s_col == jnp.where(s_row < 128, s_row, s_row + 128))
    pick_second = to_bf16(s_col == jnp.where(s_row < 128, s_row + 128, s_row + 128 + tail))
    r.padded[...] = jnp.zeros(r.padded.shape, BF16)

    def pack_own(value):
        r.padded[local : 2 * local, 0:rows] = value.astype(BF16)
        packed = nt(pick_first, r.padded[local : 3 * local, :])
        return (packed + nt(pick_second, r.padded[0 : 2 * local, :])).astype(BF16)

    got_entry()
    r.wz1[me] = pack_own(r.entry_v[...])
    pl.semaphore_wait(barrier, len(everyone))

    def to_channels(buffer):
        return [
            post(buffer.at[me], buffer.at[me], buffer.at[peer], dev(block, within, peer))
            for peer in ch_peers
        ]

    entry_waits = to_channels(r.wz1)
    got_features()
    feature_waits = [
        post(
            r.fown.at[pl.ds(per * peer, per)],
            r.fbuf.at[me],
            r.fbuf.at[peer],
            dev(block, within, peer),
        )
        for peer in ch_peers
    ]
    r.fbuf[me] = r.fown[pl.ds(per * me, per)]
    flat = jnp.concatenate([r.fown[b] for b in range(batch)], axis=1)
    wide = flat.astype(F32)
    square = wide * wide
    square_hi = square.astype(BF16)
    square_lo = (square - square_hi.astype(F32)).astype(BF16)
    level = iota((16, 256), 0)
    first_mask = jnp.concatenate([to_bf16(level == r.groups[b]) for b in range(batch)], axis=1)
    second_mask = jnp.concatenate([to_bf16(level == r.groups[b] + 4) for b in range(batch)], axis=1)
    sums = nt(first_mask, flat) + nt(second_mask, square_hi) + nt(second_mask, square_lo)

    got_affine()
    r.aff_z[me] = jnp.zeros((32, 128), F32)
    r.aff_z[me, 0 : 2 * classes + 3, 0:local] = r.affine_v[...]
    r.aff_z[me, 24:32, 0:local] = sums[0:8]
    affine_waits = to_channels(r.aff_z)

    got_exit()
    got_bypass()
    r.wz2[me, 0:hw, :] = pack_own(r.exit_v[...])
    e_row, e_col = iota((local, 128), 0), iota((local, 128), 1)
    value = r.bypass_v[...].astype(BF16)
    r.wz2[me, hw : hw + hs, :] = (
        nn(value[:hs], to_bf16(e_col == e_row)) + nn(value[hs:], to_bf16(e_col == e_row + local))
    ).astype(BF16)

    exit_waits = to_channels(r.wz2)
    got_cot()
    cotangent = Ring(
        lambda c, im: r.cown.at[per * c + im], lambda c, im: r.cbuf.at[c, im], r.pass_c
    )

    lane = iota((512, 512), 0)
    column = iota((512, 512), 1)
    spot = 256 * ((lane >> 6) & 1) + 64 * (lane >> 7) + (lane & 63)
    r.unpack[...] = to_bf16(column == spot)

    def ordered_sum(ref, size):
        result = ref[0]
        for slot in range(1, size):
            result = result + ref[slot]
        return result

    class AllReduce:
        def __init__(self, number):
            self.over_outer, self.over_inner, self.over_ch = (
                getattr(r, axis + str(number), None) for axis in "abc"
            )

        def begin(self, value):
            ref = self.over_outer
            ref[block] = value
            self.waits = [
                post(ref.at[block], ref.at[block], ref.at[peer], dev(peer, within, me))
                for peer in outer_peers
            ]

        def plane(self):
            for wait in self.waits:
                wait()
            value = ordered_sum(self.over_outer, OUTER)
            if inner > 1:
                ref = self.over_inner
                ref[within] = value
                waits = [
                    post(ref.at[within], ref.at[within], ref.at[back], dev(block, peer, me))
                    for peer, back in inner_pairs
                ]
                for wait in waits:
                    wait()
                value = ordered_sum(ref, inner)
            return value

        def middle(self):
            self.over_ch[me] = self.plane()
            self.waits = to_channels(self.over_ch)

        def end(self):
            for wait in self.waits:
                wait()
            return ordered_sum(self.over_ch, n_ch)

    def rows_of(ref, index):
        size = ref.shape[0] // OUTER
        return ref.at[pl.ds(pl.multiple_of(size * index, 16), size)]

    def unpack_own(ref, full):
        own = rows_of(ref, block)
        if full.shape[0] == hw:
            own[0:128, :] = full[0:128, 0:256]
            own[128:256, :] = full[0:128, 256:512]
            own[256 : 256 + tail, :] = full[128:, 0:256]
            own[256 + tail :, :] = full[128:, 256:512]
        else:
            own[0:hs, :] = full[:, 0:256]
            own[hs:, :] = full[:, 256:512]

    def spread(ref):
        own = rows_of(ref, block)
        return {
            mask: post(own, own, rows_of(ref, flip(block, mask)), dev(flip(block, mask), within, me))
            for mask in (2, 4, 6, 1)
        }

    def forward(ref, waits):
        rest = [waits[1]]
        for mask in (2, 4, 6):
            waits[mask]()
            mine = rows_of(ref, flip(block, mask))
            theirs = rows_of(ref, flip(partner, mask))
            rest.append(post(mine, mine, theirs, dev(partner, within, me)))
        return rest

    def widen(buffer):
        packed = jnp.concatenate([buffer[c] for c in range(n_ch)], axis=1)
        return nn(packed, r.unpack[...]).astype(BF16)

    def wide_lanes(ref):
        parts = [
            ref[c] + pltpu.roll(ref[c + 1], local, axis=1) for c in range(0, n_ch, 2)
        ]
        return jnp.concatenate(parts, axis=1)

    for wait in affine_waits:
        wait()
    affine = wide_lanes(r.aff_z)
    input_sums = AllReduce(1)
    input_sums.begin(affine[24:32])
    for wait in entry_waits:
        wait()
    unpack_own(r.w1, widen(r.wz1))
    gather1 = spread(r.w1)

    ident = to_bf16(iota((256, 256), 0) == iota((256, 256), 1))
    r.ident[...] = ident
    q_out, q_in = iota((256, 256), 0), iota((256, 256), 1)
    r.shift[0] = to_bf16((q_in == q_out + 1) & ((q_out & 15) < 15))
    r.shift[1] = to_bf16((q_in == q_out - 1) & ((q_out & 15) > 0))

    for wait in exit_waits:
        wait()
    full = widen(r.wz2)
    unpack_own(r.w2, full[0:hw])
    unpack_own(r.ws, full[hw:])
    gather2 = spread(r.w2)
    gather3 = spread(r.ws)

    rho, px = iota((512, 256), 0), iota((512, 256), 1)
    version, a, b_ = rho >> 8, (rho >> 7) & 1, (rho >> 6) & 1
    col = (rho & 15) + version * (1 - 2 * b_)
    target = (2 * ((rho & 63) >> 4) + a) * 32 + 2 * col + b_
    r.gridder[...] = to_bf16((px == target) & (col >= 0) & (col < 16))
    zeros = jnp.zeros((16, 256), BF16)
    for im in range(per):
        for ver in range(3):
            r.h1s[ver, im, 0:16, :] = zeros
            r.h1s[ver, im, 272:288, :] = zeros
        for ver in range(2):
            for ph in range(4):
                for ref in (r.h2s, r.dzs):
                    ref[ver, ph, im, 0:16, :] = zeros
                    ref[ver, ph, im, 272:288, :] = zeros

    def channel_major(ref, im, lanes):
        return jnp.concatenate([ref[c, im, :, lanes] for c in range(n_ch)], axis=0)

    for wait in feature_waits:
        wait()
    for im in range(per):
        r.fpm[256 * im : 256 * im + 256, :] = nt(
            ident, channel_major(r.fbuf, im, slice(0, 256))
        ).astype(BF16)

    stats = input_sums.plane()
    mean1 = stats[0:4] / count
    inv1 = lax.rsqrt(stats[4:8] / count - mean1 * mean1 + NORM_EPSILON)
    gain = affine[2 * classes : 2 * classes + 1]
    shift = affine[2 * classes + 1 : 2 * classes + 2]
    out_bias = affine[2 * classes + 2 : 2 * classes + 3]
    group, label, mean1_b, inv1_b, gamma_b, beta_b, mask_b = [], [], [], [], [], [], []
    for im in range(per):
        group.append(r.groups[per * me + im])
        label.append(r.labels[per * me + im])
        mean1_b.append(pick_row(mean1, group[im]))
        inv1_b.append(pick_row(inv1, group[im]))
        gamma_b.append(pick_row(affine, label[im]))
        beta_b.append(pick_row(affine, label[im] + classes))
        width = r.widths[group[im]]
        mask_b.append(
            jnp.where(iota((1, chans), 1) < width * (chans // LEVELS), 1.0, 0.0)
        )

    for im in range(per):
        normal = (r.fpm[256 * im : 256 * im + 256, :].astype(F32) - mean1_b[im]) * inv1_b[im]
        pre = gamma_b[im] * normal + beta_b[im]
        hidden = (pre * sigmoid(pre)).astype(BF16)
        r.h1s[1, im, 16:272, :] = hidden
        r.h1s[0, im, 16:272, :] = nn(r.shift[1], hidden).astype(BF16)
        r.h1s[2, im, 16:272, :] = nn(r.shift[0], hidden).astype(BF16)
        r.h1cm[:, 256 * im : 256 * im + 256] = nt(ident, hidden).astype(BF16)

    rest = forward(r.w1, gather1)
    cotangent.forward()
    for wait in rest:
        wait()

    def back_product(parts, ref):
        result = nt(parts[0], ref[0:256, :])
        for tap in range(1, 9):
            result = result + nt(parts[tap], ref[256 * tap : 256 * tap + 256, :])
        return result

    def taps():
        return [(dy, dx) for dy in range(3) for dx in range(3)]

    def stack(pieces):
        return jnp.concatenate(pieces, axis=0)

    def conv1(phase, carry):
        a, c = lax.div(phase, 2), lax.rem(phase, 2)
        parts = []
        for dy, dx in taps():
            first = pl.multiple_of(16 * lax.div(a + dy + 1, 2), 16)
            ver = lax.div(c + dx + 1, 2)
            parts.append(
                stack([r.h1s[ver, im, pl.ds(first, 256), :] for im in range(per)])
            )
        y = nn(jnp.concatenate(parts, axis=1), r.w1[...])
        r.y1[phase] = y
        out = []
        for im in range(per):
            piece = y[256 * im : 256 * im + 256]
            out.append(carry[2 * im] + colsum(piece))
            out.append(carry[2 * im + 1] + colsum(piece * piece))
        return tuple(out)

    nought = jnp.zeros((1, chans), F32)
    mid = lax.fori_loop(0, 4, conv1, (nought,) * (2 * per))
    payload = jnp.zeros((8, chans), F32)
    for im in range(per):
        payload = payload + place_row(mid[2 * im], group[im], 8)
        payload = payload + place_row(mid[2 * im + 1], group[im] + 4, 8)
    mid_sums = AllReduce(2)
    mid_sums.begin(payload)

    rest = forward(r.w2, gather2) + forward(r.ws, gather3)
    mid_sums.middle()

    r.cbuf[me] = r.cown[pl.ds(per * me, per)]
    cotangent.settle()
    for im in range(per):
        for n in range(4):
            piece = channel_major(r.cbuf, im, slice(256 * n, 256 * n + 256))
            grid = nt(r.gridder[...], piece).astype(BF16)
            for ver in range(2):
                for ph in range(4):
                    at = 256 * ver + 64 * ph
                    r.dzs[ver, ph, im, 16 + 64 * n : 80 + 64 * n, :] = grid[at : at + 64]

    coarse = jnp.zeros((256 * per, chans), F32)
    for ph in range(4):
        coarse = coarse + stack([r.dzs[0, ph, im, 16:272, :] for im in range(per)]).astype(F32)
    bias_sum = colsum(coarse)
    r.dzc[...] = coarse.astype(BF16)

    def tap_slice(ref, a, c, dy, dx, im):
        row, colm = a + dy + 1, c + dx + 1
        first = pl.multiple_of(16 * lax.div(row, 2), 16)
        ph = 2 * lax.rem(row, 2) + lax.rem(colm, 2)
        side_step = lax.div(colm, 2) - 1
        return ref[side_step * side_step, ph, im, pl.ds(first, 256), :]

    for wait in rest:
        wait()

    def back2(phase, carry):
        a, c = lax.div(phase, 2), lax.rem(phase, 2)
        parts = [
            stack([tap_slice(r.dzs, a, c, 2 - dy, 2 - dx, im) for im in range(per)])
            for dy, dx in taps()
        ]
        r.act[phase] = back_product(parts, r.w2)
        return carry

    lax.fori_loop(0, 4, back2, 0)

    stats = mid_sums.end()
    mean2 = stats[0:4] / (4.0 * count)
    inv2 = lax.rsqrt(stats[4:8] / (4.0 * count) - mean2 * mean2 + NORM_EPSILON)
    mean2_b = [pick_row(mean2, group[im]) for im in range(per)]
    inv2_b = [pick_row(inv2, group[im]) for im in range(per)]

    def hidden2(phase, carry):
        c = lax.rem(phase, 2)
        out = []
        for im in range(per):
            span = slice(256 * im, 256 * im + 256)
            normal = (r.y1[phase, span, :] - mean2_b[im]) * inv2_b[im]
            r.y1[phase, span, :] = normal
            pre = gain * normal + shift
            sig = sigmoid(pre)
            hidden = (pre * sig * mask_b[im]).astype(BF16)
            act = r.act[phase, span, :] * (sig * (1.0 + pre * (1.0 - sig)) * mask_b[im])
            r.act[phase, span, :] = act
            out.append(carry[2 * im] + colsum(act))
            out.append(carry[2 * im + 1] + colsum(act * normal))
            r.h2s[0, phase, im, 16:272, :] = hidden
            r.h2s[1, phase, im, 16:272, :] = nn(r.shift[c], hidden).astype(BF16)
            lanes = pl.ds(pl.multiple_of(512 * phase + 256 * im, 256), 256)
            r.h2cm[:, lanes] = nt(r.ident[...], hidden).astype(BF16)
        return tuple(out)

    mid = lax.fori_loop(0, 4, hidden2, (nought,) * (2 * per))
    payload = place_row(bias_sum, 8, 16)
    for im in range(per):
        payload = payload + place_row(mid[2 * im], group[im], 16)
        payload = payload + place_row(mid[2 * im + 1], group[im] + 4, 16)
    back_sums = AllReduce(3)
    back_sums.begin(payload)

    r.short[...] = nn(r.fpm[...], r.ws[...]) + out_bias
    def conv2(phase, carry):
        a, c = lax.div(phase, 2), lax.rem(phase, 2)
        parts = [
            stack([tap_slice(r.h2s, a, c, dy, dx, im) for im in range(per)]) for dy, dx in taps()
        ]
        y = nn(jnp.concatenate(parts, axis=1), r.w2[...]) + r.short[...]
        r.rc[phase] = y.astype(BF16)
        return carry

    lax.fori_loop(0, 4, conv2, 0)
    for im in range(per):
        for n in range(4):
            first = 256 * im + 64 * n
            piece = stack([r.rc[ph, first : first + 64, :] for ph in range(4)])
            r.ocm[im, :, 256 * n : 256 * n + 256] = tn(piece, r.gridder[0:256, :]).astype(BF16)

    def own_channels(ref, index, im):
        return ref.at[im, pl.ds(pl.multiple_of(local * index, local), local), :]

    def give_back(ref, out, passing):
        for im in range(per):
            out[per * me + im] = own_channels(ref, me, im)[...]
        return Ring(
            lambda c, im: own_channels(ref, c, im), lambda c, im: out.at[per * c + im], passing
        )

    back_sums.middle()
    block_output = give_back(r.ocm, r.out_v, r.pass_o)

    def grad2(tap, carry):
        dy, dx = lax.div(tap, 3), lax.rem(tap, 3)
        pieces = []
        for ph in range(4):
            a, c = ph // 2, ph % 2
            for im in range(per):
                pieces.append(tap_slice(r.dzs, a, c, 2 - dy, 2 - dx, im))
        first = pl.multiple_of(256 * tap, 256)
        r.dw2[pl.ds(first, 256), :] = nn(r.h2cm[...], stack(pieces))
        return carry

    lax.fori_loop(0, 9, grad2, 0)
    for im in range(per):
        piece = channel_major(r.fbuf, im, slice(0, 256))
        grad = nn(piece, r.dzc[256 * im : 256 * im + 256, :])
        if im == 0:
            r.dws[...] = grad
        else:
            r.dws[...] = r.dws[...] + grad

    class GradSum:
        def __init__(self, number, fetch):
            self.fetch = fetch
            self.waits = []
            for part in PARTS:
                setattr(self, part, getattr(r, part + str(number)))

        def begin(self, parts=range(4)):
            for u in parts:
                self.s1[u] = self.fetch(2 * u + 1 - core).astype(BF16)
                self.waits.append(
                    post(self.s1.at[u], self.r1.at[u], self.r1.at[u], dev(partner, within, me))
                )

        def settle(self):
            for wait in self.waits:
                wait()

        def first(self):
            self.settle()
            self.waits = []
            for mask in (6, 2, 4, 0):
                peer = flip(block, mask)
                u = lax.div(peer, 2)
                value = self.fetch(peer) + self.r1[u].astype(F32)
                if mask == 0:
                    self.r2[plane] = value.astype(BF16)
                    continue
                self.s2[u] = value.astype(BF16)
                self.waits.append(
                    post(self.s2.at[u], self.r2.at[plane], self.r2.at[u], dev(peer, within, me))
                )

        def second(self):
            self.settle()
            value = self.r2[0].astype(F32)
            for u in range(1, 4):
                value = value + self.r2[u].astype(F32)
            value = value.astype(BF16)
            left = [value[0:128], value[256 : 256 + tail]]
            right = [value[128:256], value[256 + tail : rows]]
            if value.shape[0] > rows:
                left.append(value[rows : rows + hs])
                right.append(value[rows + hs :])
            pair = jnp.concatenate([stack(left), stack(right)], axis=1)
            packed = nt(pair, r.unpack[...]).astype(BF16)
            for c in range(n_ch):
                self.s3[c] = packed[:, 128 * c : 128 * c + 128]
            self.r3[me] = self.s3[me]
            self.waits = [
                post(self.s3.at[peer], self.r3.at[me], self.r3.at[peer], dev(block, within, peer))
                for peer in ch_peers
            ]

        def end(self, out, out_small=None):
            self.settle()
            done = self.r3[0].astype(F32)
            for c in range(1, n_ch):
                done = done + self.r3[c].astype(F32)
            turned = done[0:128].T
            out[:, 0:128] = turned[0:local]
            out[:, 128:256] = turned[local:]
            gap = jnp.zeros((128 - tail, 128), F32)
            turned = stack([done[128 : 128 + tail], gap]).T
            ends = turned[0:local] + pltpu.roll(turned[local:], tail, axis=1)
            out[:, 256:rows] = ends[:, 0 : rows - 256]
            if out_small is not None:
                last = done[hw:]
                out_small[0:hs, :] = last[:, 0:local]
                out_small[hs:, :] = pltpu.roll(last, local, axis=1)[:, 0:local]

    def block_rows(ref, size, index):
        return ref[pl.ds(pl.multiple_of(size * index, 8), size), :]

    second = GradSum(2, lambda k: stack([block_rows(r.dw2, rows, k), block_rows(r.dws, small, k)]))
    entry = GradSum(1, lambda k: block_rows(r.dw1, rows, k))
    second.begin()
    r.dshort[...] = nt(r.dzc[...], r.ws[...])

    stats = back_sums.end()
    affine_grad2 = stats
    p1_b = [pick_row(stats[0:4], group[im]) / (4.0 * count) for im in range(per)]
    p2_b = [pick_row(stats[4:8], group[im]) / (4.0 * count) for im in range(per)]

    for im in range(per):
        span = slice(256 * im, 256 * im + 256)
        scale = gain * inv2_b[im]
        combos = []
        for a in range(2):
            grads = []
            for c in range(2):
                ph = 2 * a + c
                d = scale * (r.act[ph, span, :] - (p1_b[im] + r.y1[ph, span, :] * p2_b[im]))
                grads.append(d.astype(BF16))
            right = nn(r.shift[0], grads[0])
            left = nn(r.shift[1], grads[1])
            even, odd = grads[0].astype(F32), grads[1].astype(F32)
            combos.append((odd + right, even + odd, left + even))
        gap = jnp.zeros((16, chans), F32)
        for dx in range(3):
            upper, lower = combos[0][dx], combos[1][dx]
            r.field[dx, im] = (lower + stack([upper[16:], gap])).astype(BF16)
            r.field[3 + dx, im] = (upper + lower).astype(BF16)
            r.field[6 + dx, im] = (stack([gap, lower[:-16]]) + upper).astype(BF16)

    second.first()
    block_output.forward()

    def grad1(tap, carry):
        first = pl.multiple_of(256 * tap, 256)
        r.dw1[pl.ds(first, 256), :] = nn(
            r.h1cm[...], stack([r.field[tap, im] for im in range(per)])
        )
        return carry

    for u, (first, last) in enumerate(((0, 3), (3, 5), (5, 7), (7, 9))):
        lax.fori_loop(first, last, grad1, 0)
        entry.begin([u])

    parts = [stack([r.field[tap, im] for im in range(per)]) for tap in range(9)]
    dh1 = back_product(parts, r.w1)
    payload = jnp.zeros((8, chans), F32)
    class_rows = jnp.zeros((24, chans), F32)
    for im in range(per):
        span = slice(256 * im, 256 * im + 256)
        normal = (r.fpm[span, :].astype(F32) - mean1_b[im]) * inv1_b[im]
        pre = gamma_b[im] * normal + beta_b[im]
        sig = sigmoid(pre)
        act = dh1[span] * (sig * (1.0 + pre * (1.0 - sig)))
        r.act1[span, :] = act
        q1, q2 = colsum(act), colsum(act * normal)
        class_rows = class_rows + place_row(q2, label[im], 24)
        class_rows = class_rows + place_row(q1, label[im] + classes, 24)
        payload = payload + place_row(gamma_b[im] * q1, group[im], 8)
        payload = payload + place_row(gamma_b[im] * q2, group[im] + 4, 8)
    last_sums, class_sums = AllReduce(4), AllReduce(6)
    last_sums.begin(payload)
    entry.first()
    class_sums.begin(class_rows)
    last_sums.middle()
    second.second()
    stats = last_sums.end()
    for im in range(per):
        span = slice(256 * im, 256 * im + 256)
        normal = (r.fpm[span, :].astype(F32) - mean1_b[im]) * inv1_b[im]
        r1 = pick_row(stats[0:4], group[im]) / count
        r2 = pick_row(stats[4:8], group[im]) / count
        grad = inv1_b[im] * (gamma_b[im] * r.act1[span, :] - (r1 + normal * r2))
        grad = (grad + r.dshort[span, :]).astype(BF16)
        r.dcm[im] = nt(r.ident[...], grad).astype(BF16)
    entry.second()
    input_gradient = give_back(r.dcm, r.dx_v, r.pass_x)
    class_sums.middle()
    second.end(r.grad2, r.grad3)

    row = iota((8, 128), 0)

    def norm_rows(index, weight, grad, v):
        for wait in held[index]:
            wait()
        master = weight[...]
        _, _, direction = adam_update(
            grad[...], getattr(r, v + "m")[...], getattr(r, v + "q")[...]
        )
        update = direction + WEIGHT_DECAY * master
        rows_w = jnp.where(row == index, total(master * master), 0.0)
        return rows_w + jnp.where(row == index + 3, total(update * update), 0.0)

    if inner == 1:
        norms = norm_rows(1, r.exit_v, r.grad2, "v2") + norm_rows(2, r.bypass_v, r.grad3, "vs")

    if inner == 1:
        entry.end(r.grad1)
        norms = norms + norm_rows(0, r.entry_v, r.grad1, "v1")
        norm_sums = AllReduce(5)
        norm_sums.begin(norms)
        input_gradient.forward()
        norm_sums.middle()
    else:
        entry.end(r.grad1)
        input_gradient.forward()
        r.norms[...] = jnp.zeros((8, 128), F32)

    table = jnp.zeros((24, chans), F32)
    table = table + jnp.where(iota((24, chans), 0) < 2 * classes, class_sums.end(), 0.0)
    table = table + place_row(colsum(affine_grad2[4:8]), 2 * classes, 24)
    table = table + place_row(colsum(affine_grad2[0:4]), 2 * classes + 1, 24)
    table = table + place_row(affine_grad2[8:9], 2 * classes + 2, 24)
    mine = jnp.zeros((24, 128), F32)
    for c in range(n_ch):
        piece = table[:, 128 * (c // 2) : 128 * (c // 2) + 128]
        if c % 2:
            piece = pltpu.roll(piece, local, axis=1)
        mine = mine + jnp.where(me == c, piece, 0.0)
    r.affine_grad[...] = mine

    block_output.settle()
    written = [here(r.out_v, r.out)]
    input_gradient.settle()
    written.append(here(r.dx_v, r.dx))
    if inner == 1:
        r.norms[...] = norm_sums.end()
    for wait in written:
        wait()
    for wait in pending:
        wait()
    cfg.used.append((slots.remote, slots.local))


def final_kernel(cfg, *refs):
    r = SimpleNamespace(**dict(zip(cfg.names, refs)))
    classes = cfg.classes
    local = cfg.local
    r.block_output[...] = r.out[...]
    r.input_gradient[...] = r.dx[...].astype(F32)
    norms = jnp.sqrt(r.norms[...])
    weight_norm, update_norm = norms[0:3, 0:1], norms[3:6, 0:1]
    ratio = weight_norm / update_norm
    at = iota((3, 3), 1)
    r.trust_norms[...] = jnp.where(
        at == 0, weight_norm, jnp.where(at == 1, update_norm, ratio)
    )
    sets = (
        (r.entry, r.entry_m, r.entry_q, r.entry_g, r.entry_1, r.entry_2, r.entry_w),
        (r.exit, r.exit_m, r.exit_q, r.exit_g, r.exit_1, r.exit_2, r.exit_w),
        (r.bypass, r.bypass_m, r.bypass_q, r.bypass_g, r.bypass_1, r.bypass_2, r.bypass_w),
    )
    for index, (weight, m, q, g, first, second, result) in enumerate(sets):
        master = weight[...]
        moment, square, direction = adam_update(g[...], m[...], q[...])
        update = direction + WEIGHT_DECAY * master
        first[...] = moment
        second[...] = square
        result[...] = master - MATRIX_RATE * ratio[index : index + 1] * update
    grad = r.affine_grad[0 : 2 * classes + 3, 0:local]
    moment, square, direction = adam_update(grad, r.affine_m[...], r.affine_q[...])
    r.affine_1[...] = moment
    r.affine_2[...] = square
    r.affine_w[...] = r.affine[...] - AFFINE_RATE * direction


def per_device(
    features,
    labels,
    groups,
    widths,
    entry_conv,
    entry_moment,
    entry_square,
    exit_conv,
    exit_moment,
    exit_square,
    bypass_conv,
    bypass_moment,
    bypass_square,
    norm_affine,
    norm_moment,
    norm_square,
    cotangent,
):
    n_img, n_ch = lax.axis_size("img"), lax.axis_size("ch")
    batch, local, pixels = features.shape
    chans = local * n_ch
    side = math.isqrt(pixels)
    inner = n_img // OUTER
    classes = (norm_affine.shape[0] - 3) // 2
    per = batch // n_ch
    assert (side, chans, n_ch, local, batch % n_ch) == (16, 256, 4, 64, 0) and per == 2
    rows, small = entry_conv.shape[0] * inner, bypass_conv.shape[0] * inner
    masters = (entry_conv, exit_conv, bypass_conv)
    if inner == 1:
        blocks = masters
    else:
        sets = [[o * inner + i for i in range(inner)] for o in range(OUTER)]
        blocks = tuple(
            lax.all_gather(w.astype(BF16), "img", axis=0, tiled=True, axis_index_groups=sets)
            for w in masters
        )

    vmem = pl.BlockSpec(memory_space=pltpu.VMEM)
    smem = pl.BlockSpec(memory_space=pltpu.SMEM)
    anywhere = pl.BlockSpec(memory_space=pl.ANY)
    states = dict(
        entry_m=entry_moment.T,
        entry_q=entry_square.T,
        exit_m=exit_moment.T,
        exit_q=exit_square.T,
        bypass_m=bypass_moment,
        bypass_q=bypass_square,
    )
    inputs = dict(
        labels=(labels, smem),
        groups=(groups, smem),
        widths=(widths, smem),
        features=(features, anywhere),
        cotangent=(cotangent, anywhere),
        entry=(blocks[0].T, anywhere),
        exit=(blocks[1].T, anywhere),
        bypass=(blocks[2], anywhere),
        affine=(norm_affine, anywhere),
    )
    if inner == 1:
        inputs.update({name: (value, anywhere) for name, value in states.items()})
    sds = jax.ShapeDtypeStruct
    outputs = dict(
        out=(sds(cotangent.shape, BF16), anywhere),
        dx=(sds(features.shape, BF16), anywhere),
        grad1=(sds((local, rows), F32), vmem),
        grad2=(sds((local, rows), F32), vmem),
        grad3=(sds((small, local), F32), vmem),
        affine_grad=(sds((24, 128), F32), vmem),
        norms=(sds((8, 128), F32), vmem),
    )
    pix = pixels * per
    taps9 = 9 * chans
    held = lambda shape, dtype=BF16: pltpu.VMEM(shape, dtype)
    scratch = dict(
        fown=held((batch, local, pixels)),
        cown=held((batch, local, 4 * pixels)),
        pass_c=held((2, local, 4 * pixels)),
        pass_o=held((2, local, 4 * pixels)),
        pass_x=held((2, local, pixels)),
        out_v=held(cotangent.shape),
        dx_v=held(features.shape),
        fbuf=held((n_ch, per, local, pixels)),
        cbuf=held((n_ch, per, local, 4 * pixels)),
        entry_v=held((local, rows), blocks[0].dtype),
        exit_v=held((local, rows), blocks[1].dtype),
        bypass_v=held((small, local), blocks[2].dtype),
        affine_v=held(norm_affine.shape, F32),
        padded=held((3 * local, 384)),
        wz1=held((n_ch, rows // 2, 128)),
        wz2=held((n_ch, (rows + small) // 2, 128)),
        aff_z=held((n_ch, 32, 128), F32),
        w1=held((taps9, chans)),
        w2=held((taps9, chans)),
        ws=held((chans, chans)),
        unpack=held((512, 512)),
        ident=held((256, 256)),
        shift=held((2, 256, 256)),
        gridder=held((512, 256)),
        fpm=held((pix, chans)),
        h1s=held((3, per, pixels + 32, chans)),
        h1cm=held((chans, pix)),
        y1=held((4, pix, chans), F32),
        act=held((4, pix, chans), F32),
        h2s=held((2, 4, per, pixels + 32, chans)),
        dzs=held((2, 4, per, pixels + 32, chans)),
        h2cm=held((chans, 4 * pix)),
        short=held((pix, chans), F32),
        dshort=held((pix, chans), F32),
        dzc=held((pix, chans)),
        act1=held((pix, chans), F32),
        rc=held((4, pix, chans)),
        ocm=held((per, chans, 4 * pixels)),
        dcm=held((per, chans, pixels)),
        field=held((9, per, pixels, chans)),
        dw1=held((taps9, chans), F32),
        dw2=held((taps9, chans), F32),
        dws=held((chans, chans), F32),
    )
    for number, size in ((1, rows), (2, rows + small)):
        shapes = ((4, size, chans),) * 4 + ((n_ch, size // 2, 128),) * 2
        for part, shape in zip(PARTS, shapes):
            scratch[part + str(number)] = held(shape)
    exchanges = [(8, chans), (8, chans), (16, chans), (8, chans), (8, 128), (24, chans)]
    if inner == 1:
        for v, shape in (("v1", (local, rows)), ("v2", (local, rows)), ("vs", (small, local))):
            scratch[v + "m"] = held(shape, F32)
            scratch[v + "q"] = held(shape, F32)
    for number, shape in enumerate(exchanges, 1):
        for axis, size in zip("abc", (OUTER, inner, n_ch)):
            if size > 1:
                scratch[axis + str(number)] = held((size,) + shape, F32)
    remote_count = 3 * 3 + 4 * 4 * per + 3 * 7 + 2 * 13 + len(exchanges) * (7 + 3 + inner - 1)
    scratch.update(
        send=pltpu.SemaphoreType.DMA((remote_count,)),
        recv=pltpu.SemaphoreType.DMA((remote_count,)),
        lsem=pltpu.SemaphoreType.DMA((20,)),
    )
    cfg = SimpleNamespace(
        names=[*inputs, *outputs, *scratch],
        inner=inner,
        n_ch=n_ch,
        batch=batch,
        local=local,
        classes=classes,
        count=float(batch * n_img // widths.shape[0] * pixels),
        rows=rows,
        small=small,
        used=[],
    )
    out, dx, grad1, grad2, grad3, affine_grad, norms = pl.pallas_call(
        functools.partial(main_kernel, cfg),
        out_shape=[s for s, _ in outputs.values()],
        in_specs=[s for _, s in inputs.values()],
        out_specs=[s for _, s in outputs.values()],
        scratch_shapes=list(scratch.values()),
        compiler_params=pltpu.CompilerParams(
            collective_id=0, has_side_effects=True, vmem_limit_bytes=VMEM_LIMIT
        ),
        name="block_step",
    )(*[v for v, _ in inputs.values()])
    assert max(n for n, _ in cfg.used) <= remote_count and max(n for _, n in cfg.used) <= 20

    grads = [grad1, grad2, grad3]
    if inner > 1:
        grads = [
            lax.psum_scatter(g, "img", scatter_dimension=0, axis_index_groups=sets, tiled=True)
            for g in (grad1.T, grad2.T, grad3)
        ]
        updates = []
        for w, g, m, s in zip(
            masters,
            grads,
            (entry_moment, exit_moment, bypass_moment),
            (entry_square, exit_square, bypass_square),
        ):
            updates.append(adam_update(g, m, s)[2] + WEIGHT_DECAY * w)
        sums = lax.psum(
            jnp.stack([jnp.sum(w * w) for w in masters] + [jnp.sum(u * u) for u in updates]),
            ("img", "ch"),
        )
        norms = jnp.broadcast_to(jnp.pad(sums, (0, 2))[:, None], (8, 128))
        grads = [grads[0].T, grads[1].T, grads[2]]

    args = dict(
        out=out,
        dx=dx,
        norms=norms,
        affine_grad=affine_grad,
        entry_g=grads[0],
        exit_g=grads[1],
        bypass_g=grads[2],
        entry=entry_conv.T,
        exit=exit_conv.T,
        bypass=bypass_conv,
        **states,
        affine=norm_affine,
        affine_m=norm_moment,
        affine_q=norm_square,
    )
    tall = sds(entry_conv.shape[::-1], F32)
    short, wide = (sds(w.shape, F32) for w in (bypass_conv, norm_affine))
    results = dict(
        block_output=sds(cotangent.shape, BF16),
        input_gradient=sds(features.shape, F32),
        entry_1=tall,
        entry_2=tall,
        entry_w=tall,
        exit_1=tall,
        exit_2=tall,
        exit_w=tall,
        bypass_1=short,
        bypass_2=short,
        bypass_w=short,
        affine_1=wide,
        affine_2=wide,
        affine_w=wide,
        trust_norms=sds((3, 3), F32),
    )
    end_cfg = SimpleNamespace(names=[*args, *results], classes=classes, local=local)
    final = pl.pallas_call(
        functools.partial(final_kernel, end_cfg),
        out_shape=list(results.values()),
        in_specs=[vmem] * len(args),
        out_specs=[vmem] * len(results),
        compiler_params=pltpu.CompilerParams(vmem_limit_bytes=VMEM_LIMIT),
        name="finish",
    )(*args.values())
    return tuple(v.T if s is tall else v for v, s in zip(final, results.values()))


def solution(mesh):
    wide = P("img", "ch")
    deep = P("img", "ch", None)
    table = P(None, "ch")
    return jax.shard_map(
        per_device,
        mesh=mesh,
        in_specs=(deep, P("img"), P("img"), P()) + (wide,) * 9 + (table,) * 3 + (deep,),
        out_specs=(deep, deep) + (wide,) * 9 + (table,) * 3 + (P(),),
        check_vma=False,
    )
```

profile of v0, /device:TPU:0, one launch (start us, length us, event | category | flops | bytes accessed | tf_op | source)
XLA Modules:
  0.0 104.1 jit_solution(14945120713320436985)
XLA Ops:
  0.6 100.3 %block_step.1 = (bf16[8,64,1024]{2,1,0:T(8,128)(2,1)}, bf16[8,64,256]{2,1,0:T(8,128)(2,1)}, f32[64,288]{1,0:T(8,128)}, f32[64,288]{1,0:T(8,128)}, f32[32,64]{1,0...) custom-call(s32[8]{0:T(128)} %refs_0_.1, s32[8]{0:T(128)} %refs_1_.1, s32[4]{0:T(128)} %refs_2_.1, ...), custom_call_target="tpu_custom_call" | custom-call | tf_op jit(solution)/shard_map/block_step/pallas_call | solution.py:995
  101.0 3.1 %finish.1 = (bf16[8,64,1024]{2,1,0:T(8,128)(2,1)}, f32[8,64,256]{2,1,0:T(8,128)}, f32[64,288]{1,0:T(8,128)}, f32[64,288]{1,0:T(8,128)}, f32[64,288]{1,0:T(8,128)...) custom-call(bf16[8,64,1024]{2,1,0:T(8,128)(2,1)} %get-tuple-element., ...), custom_call_target="tpu_custom_call" | custom-call | tf_op jit(solution)/shard_map/finish/pallas_call | solution.py:1065
where the time goes:
time: 104 us
  Pallas kernels  103 us (99%)
    pallas_call x1, Pallas kernels, per_device(): pl.pallas_call(functools.partial(main_kernel, cfg), out_shape=[s for s, _...  100 us
    pallas_call x1, Pallas kernels, per_device(): pl.pallas_call(functools.partial(final_kernel, end_cfg), out_shape=list(r...  3.12 us

commit v1 on v0

--- a/solution.py
+++ b/solution.py
@@ -430,8 +430,9 @@
         r.h1s[0, im, 16:272, :] = nn(r.shift[1], hidden).astype(BF16)
         r.h1s[2, im, 16:272, :] = nn(r.shift[0], hidden).astype(BF16)
         r.h1cm[:, 256 * im : 256 * im + 256] = nt(ident, hidden).astype(BF16)
-
-    rest = forward(r.w1, gather1)
+        if im == 0:
+            rest = forward(r.w1, gather1)
+
     cotangent.forward()
     for wait in rest:
         wait()
@@ -591,7 +592,6 @@
         r.dw2[pl.ds(first, 256), :] = nn(r.h2cm[...], stack(pieces))
         return carry
 
-    lax.fori_loop(0, 9, grad2, 0)
     for im in range(per):
         piece = channel_major(r.fbuf, im, slice(0, 256))
         grad = nn(piece, r.dzc[256 * im : 256 * im + 256, :])
@@ -676,9 +676,9 @@
 
     second = GradSum(2, lambda k: stack([block_rows(r.dw2, rows, k), block_rows(r.dws, small, k)]))
     entry = GradSum(1, lambda k: block_rows(r.dw1, rows, k))
-    second.begin()
-    r.dshort[...] = nt(r.dzc[...], r.ws[...])
-
+    for u, (first, last) in enumerate(((0, 3), (3, 5), (5, 7), (7, 9))):
+        lax.fori_loop(first, last, grad2, 0)
+        second.begin([u])
     stats = back_sums.end()
     affine_grad2 = stats
     p1_b = [pick_row(stats[0:4], group[im]) / (4.0 * count) for im in range(per)]
@@ -741,6 +741,7 @@
     class_sums.begin(class_rows)
     last_sums.middle()
     second.second()
+    r.dshort[...] = nt(r.dzc[...], r.ws[...])
     stats = last_sums.end()
     for im in range(per):
         span = slice(256 * im, 256 * im + 256)

time: 104 us -> 104 us (level)
  no operation moved by 1% of the time
where the time goes in v1:
time: 104 us
  Pallas kernels  103 us (99%)
    pallas_call x1, Pallas kernels, per_device(): pl.pallas_call(functools.partial(main_kernel, cfg), out_shape=[s for s, _...  100 us
    pallas_call x1, Pallas kernels, per_device(): pl.pallas_call(functools.partial(final_kernel, end_cfg), out_shape=list(r...  3.12 us

profile of v1, /device:TPU:0, one launch (start us, length us, event | category | flops | bytes accessed | tf_op | source)
XLA Modules:
  0.0 104.2 jit_solution(3090751756335537905)
XLA Ops:
  0.6 100.3 %block_step.1 = (bf16[8,64,1024]{2,1,0:T(8,128)(2,1)}, bf16[8,64,256]{2,1,0:T(8,128)(2,1)}, f32[64,288]{1,0:T(8,128)}, f32[64,288]{1,0:T(8,128)}, f32[32,64]{1,0...) custom-call(s32[8]{0:T(128)} %refs_0_.1, s32[8]{0:T(128)} %refs_1_.1, s32[4]{0:T(128)} %refs_2_.1, ...), custom_call_target="tpu_custom_call" | custom-call | tf_op jit(solution)/shard_map/block_step/pallas_call | solution.py:996
  101.0 3.1 %finish.1 = (bf16[8,64,1024]{2,1,0:T(8,128)(2,1)}, f32[8,64,256]{2,1,0:T(8,128)}, f32[64,288]{1,0:T(8,128)}, f32[64,288]{1,0:T(8,128)}, f32[64,288]{1,0:T(8,128)...) custom-call(bf16[8,64,1024]{2,1,0:T(8,128)(2,1)} %get-tuple-element., ...), custom_call_target="tpu_custom_call" | custom-call | tf_op jit(solution)/shard_map/finish/pallas_call | solution.py:1066

commit v2 on v1

--- a/solution.py
+++ b/solution.py
@@ -221,15 +221,6 @@
 
     entry_waits = to_channels(r.wz1)
     got_features()
-    feature_waits = [
-        post(
-            r.fown.at[pl.ds(per * peer, per)],
-            r.fbuf.at[me],
-            r.fbuf.at[peer],
-            dev(block, within, peer),
-        )
-        for peer in ch_peers
-    ]
     r.fbuf[me] = r.fown[pl.ds(per * me, per)]
     flat = jnp.concatenate([r.fown[b] for b in range(batch)], axis=1)
     wide = flat.astype(F32)
@@ -246,6 +237,15 @@
     r.aff_z[me, 0 : 2 * classes + 3, 0:local] = r.affine_v[...]
     r.aff_z[me, 24:32, 0:local] = sums[0:8]
     affine_waits = to_channels(r.aff_z)
+    feature_waits = [
+        post(
+            r.fown.at[pl.ds(per * peer, per)],
+            r.fbuf.at[me],
+            r.fbuf.at[peer],
+            dev(block, within, peer),
+        )
+        for peer in ch_peers
+    ]
 
     got_exit()
     got_bypass()
@@ -742,6 +742,7 @@
     last_sums.middle()
     second.second()
     r.dshort[...] = nt(r.dzc[...], r.ws[...])
+    entry.second()
     stats = last_sums.end()
     for im in range(per):
         span = slice(256 * im, 256 * im + 256)
@@ -751,7 +752,6 @@
         grad = inv1_b[im] * (gamma_b[im] * r.act1[span, :] - (r1 + normal * r2))
         grad = (grad + r.dshort[span, :]).astype(BF16)
         r.dcm[im] = nt(r.ident[...], grad).astype(BF16)
-    entry.second()
     input_gradient = give_back(r.dcm, r.dx_v, r.pass_x)
     class_sums.middle()
     second.end(r.grad2, r.grad3)

time: 104 us -> 105 us (level)
  no operation moved by 1% of the time
where the time goes in v2:
time: 105 us
  Pallas kernels  104 us (99%)
    pallas_call x1, Pallas kernels, per_device(): pl.pallas_call(functools.partial(main_kernel, cfg), out_shape=[s for s, _...  101 us
    pallas_call x1, Pallas kernels, per_device(): pl.pallas_call(functools.partial(final_kernel, end_cfg), out_shape=list(r...  3.12 us

profile of v2, /device:TPU:0, one launch (start us, length us, event | category | flops | bytes accessed | tf_op | source)
XLA Modules:
  0.0 105.1 jit_solution(3658174396987521402)
XLA Ops:
  0.6 101.2 %block_step.1 = (bf16[8,64,1024]{2,1,0:T(8,128)(2,1)}, bf16[8,64,256]{2,1,0:T(8,128)(2,1)}, f32[64,288]{1,0:T(8,128)}, f32[64,288]{1,0:T(8,128)}, f32[32,64]{1,0...) custom-call(s32[8]{0:T(128)} %refs_0_.1, s32[8]{0:T(128)} %refs_1_.1, s32[4]{0:T(128)} %refs_2_.1, ...), custom_call_target="tpu_custom_call" | custom-call | tf_op jit(solution)/shard_map/block_step/pallas_call | solution.py:996
  101.8 3.1 %finish.1 = (bf16[8,64,1024]{2,1,0:T(8,128)(2,1)}, f32[8,64,256]{2,1,0:T(8,128)}, f32[64,288]{1,0:T(8,128)}, f32[64,288]{1,0:T(8,128)}, f32[64,288]{1,0:T(8,128)...) custom-call(bf16[8,64,1024]{2,1,0:T(8,128)(2,1)} %get-tuple-element., ...), custom_call_target="tpu_custom_call" | custom-call | tf_op jit(solution)/shard_map/finish/pallas_call | solution.py:1066
